TPU v7x, 512 devices: a whole 4x4x16 slice. The times are simulated.
512 devices in a mesh: dp: 64 (over z_lo, x, core), tensor: 8 (over z_hi, y).
Axes of the slice: x: 4, y: 4, z: 16 (z_hi: 2, z_lo: 8; z = z_hi * 8 + z_lo), core: 2. Of those that a mesh axis runs over, the one named last changes fastest.
Arguments:
- language: int32 [64], replicated, may hold values from 0 to 3, as said below
- hidden: bfloat16 [16384, 5632], P('dp', 'tensor'), may hold values from -6 to 6
- context: bfloat16 [16384, 2048], P('dp', 'tensor'), may hold values from -3 to 3
- grad_out: bfloat16 [16384, 4096], P(('dp', 'tensor')), may hold values from -3 to 3
Outputs:
- module_grad: bfloat16 [4, 5632, 4096], P(None, 'tensor', 'dp')
- attention_grad: float32 [4096, 2048], P('dp', 'tensor')
Inputs may be any that keep to these rules, and one draw needn't show every extreme that they name: Every language of 0 to 3 belongs to at least one replica; no language has more than 25 replicas.
All inputs are finite; a program needn't handle non-finite values.
Results may differ from a plain program's by a relative error of at most 0.0049.
Values may be sent and summed in bfloat16 or wider, within the bound.
A program may use at most 64 MiB of HBM per device.

v0:
```python
import jax
import jax.numpy as jnp
from jax import lax
from jax.sharding import PartitionSpec as P

LANGS = 4


def contract_rows(left, right):
    return lax.dot_general(
        left, right, (((0,), (0,)), ((), ())), preferred_element_type=jnp.float32
    )


def module_part(language, hidden, gathered):
    product = contract_rows(hidden, gathered).astype(jnp.bfloat16)
    received = lax.all_to_all(product[None], "dp", split_axis=2, concat_axis=0, tiled=True)
    lang_range = jnp.arange(LANGS, dtype=jnp.int32)
    selector = (language[:, None] == lang_range[None, :]).astype(jnp.bfloat16)
    summed = contract_rows(selector, received)
    return summed.astype(jnp.bfloat16)


def attention_part(context, gathered):
    full_sum = contract_rows(gathered, context)
    return lax.psum_scatter(full_sum, "dp", scatter_dimension=0, tiled=True)


def shards(language, hidden, context, grad_out):
    gathered = lax.all_gather(grad_out, "tensor", axis=0, tiled=True)
    module_grad = module_part(language, hidden, gathered)
    attention_grad = attention_part(context, gathered)
    return (module_grad, attention_grad)


def solution(mesh):
    placed = (P(), P("dp", "tensor"), P("dp", "tensor"), P(("dp", "tensor"), None))
    return jax.shard_map(
        shards,
        mesh=mesh,
        in_specs=placed,
        out_specs=(P(None, "tensor", "dp"), P("dp", "tensor")),
        check_vma=False,
    )
```

profile of v0, /device:TPU:1, one launch (start us, length us, event | category | flops | bytes accessed | tf_op | source)
XLA Modules:
  0.0 713.4 jit_solution(12589394136122702870)
XLA Ops:
  7.2 0.0 copy-start
  7.2 0.0 all-gather.2.cloned.1.call-start
  7.2 0.7 all-gather.2.cloned.1.call-update
  7.9 125.5 %all-gather.2.cloned.1.call-done = bf16[256,4096]{1,0:T(8,128)(2,1)} async-done(((bf16[32,4096]{1,0:T(8,128)(2,1)}), bf16[256,4096]{1,0:T(8,128)(2,1)}) %all-gather.2.cloned.1.call-update) | async-done | bytes 2097168 | tf_op jit(solution)/shard_map/all_gather | solution.py:30
  133.4 0.0 copy-done
  133.4 5.7 fusion.3
  139.1 27.6 %copy.11 = bf16[1,704,4096]{1,0,2:T(2,128)(2,1)} copy(bf16[1,704,4096]{2,1,0:T(8,128)(2,1)} %fusion.3) | data formatting | bytes 11534336 | tf_op jit(solution)/shard_map/broadcast_in_dim | solution.py:17
  166.7 0.5 broadcast.1
  167.2 70.4 %reduce = bf16[4096,704]{1,0:T(8,128)(2,1)} reduce(bf16[4096,1,704]{2,1,0:T(2,128)(2,1)} %bitcast.20, bf16[]{:T(256)} %broadcast.1), dimensions={1}, to_apply=%bitcast.13.reduce_sub_computation | reduce | bytes 11534338
  237.6 15.5 %reshape.6 = bf16[64,2,22528]{2,1,0:T(2,128)(2,1)} reshape(bf16[4096,704]{1,0:T(8,128)(2,1)} %reduce) | data formatting | bytes 11534336
  253.1 0.0 copy-start.1
  253.1 0.0 copy-start.2
  253.1 9.8 %all-to-all-start = ((bf16[64,2,22528]{2,1,0:T(2,128)(2,1)}), bf16[64,2,22528]{2,1,0:T(2,128)(2,1)}, u32[]{:S(2)}, u32[]{:S(2)}) async-start(bf16[64,2,22528]{2,1,0:T(2,128)(2,1)} %reshape.6), calls=%async_computation | async-start | bytes 11534336 | tf_op jit(solution)/shard_map/all_to_all | solution.py:17
  262.9 0.2 reduce-scatter.2.cloned.1.call-start
  263.1 0.0 copy-done.1
  263.1 0.0 copy-done.2
  263.1 2.8 fusion.10
  265.9 0.0 reduce-scatter.2.cloned.1.call-update
  265.9 260.4 %all-to-all-done = bf16[64,2,22528]{2,1,0:T(2,128)(2,1)} async-done(((bf16[64,2,22528]{2,1,0:T(2,128)(2,1)}), bf16[64,2,22528]{2,1,0:T(2,128)(2,1)}, u32[]{:S(2)}, u32[]{:S(2)}) %all-to-all-start) | async-done | bytes 5767200 | tf_op jit(solution)/shard_map/all_to_all | solution.py:17
  526.3 38.6 %reshape.7 = bf16[4096,1,704]{2,1,0:T(2,128)(2,1)} reshape(bf16[64,2,22528]{2,1,0:T(2,128)(2,1)} %all-to-all-done) | data formatting | bytes 11534336
  564.9 0.0 copy-start.3
  564.9 5.7 copy.14
  570.6 0.0 copy-done.3
  570.6 6.7 fusion.4
  577.3 0.8 copy.13
  578.1 128.4 %reduce-scatter.2.cloned.1.call-done = f32[64,256]{1,0:T(8,128)} async-done(((f32[4096,256]{1,0:T(8,128)}), f32[64,256]{1,0:T(8,128)}) %reduce-scatter.2.cloned.1.call-update) | async-done | bytes 65552 | tf_op jit(solution)/shard_map/reduce_scatter | solution.py:26
Async XLA Ops:
  7.2 126.2 %copy-start = (bf16[256,704]{0,1:T(8,128)(2,1)S(1)}, bf16[256,704]{0,1:T(8,128)(2,1)}, u32[]{:S(2)}) copy-start(bf16[256,704]{0,1:T(8,128)(2,1)} %param.5) | copy-start | bytes 1081348
  7.2 126.2 %all-gather.2.cloned.1.call-start = ((), (), s32[]{:S(2)}) async-start(), calls=%async_computation.2 | async-start | bytes 2359296 | tf_op jit(solution)/shard_map/all_gather | solution.py:30
  253.1 10.0 %copy-start.1 = (bf16[256,4096]{1,0:T(8,128)(2,1)S(1)}, bf16[256,4096]{1,0:T(8,128)(2,1)}, u32[]{:S(2)}) copy-start(bf16[256,4096]{1,0:T(8,128)(2,1)} %all-gather.2.cloned.1.call-done) | copy-start | bytes 6291460
  253.1 10.0 %copy-start.2 = (bf16[256,256]{1,0:T(8,128)(2,1)S(1)}, bf16[256,256]{1,0:T(8,128)(2,1)}, u32[]{:S(2)}) copy-start(bf16[256,256]{1,0:T(8,128)(2,1)} %param.6) | copy-start | bytes 393220
  253.1 273.2 %all-to-all-start = ((bf16[64,2,22528]{2,1,0:T(2,128)(2,1)}), bf16[64,2,22528]{2,1,0:T(2,128)(2,1)}, u32[]{:S(2)}, u32[]{:S(2)}) async-start(bf16[64,2,22528]{2,1,0:T(2,128)(2,1)} %reshape.6), calls=%async_computation | async-start | bytes 11534336 | tf_op jit(solution)/shard_map/all_to_all | solution.py:17
  262.9 443.6 %reduce-scatter.2.cloned.1.call-start = ((), (), s32[]{:S(2)}) async-start(), calls=%async_computation.3 | async-start | bytes 4259840 | tf_op jit(solution)/shard_map/reduce_scatter | solution.py:26
  564.9 5.7 copy-start.3
Sparse Core Ops, SparseCore 0:
  11.2 122.1 all-gather.1
  267.1 439.3 reduce-scatter.1
where the time goes:
time: 726 us; the launch traced here: 713 us
  waiting for transfers between devices  515 us (71%)
  local copies, waits for them, and re-layouts  88.7 us (12%)
  other arithmetic  70.4 us (10%)
  matrix products  15.2 us (2%)
  between operations  14.1 us (2%)
  starting transfers between devices  10 us (1%)
    all_to_all x1, waiting for transfers between devices, module_part(): lax.all_to_all(product[None], 'dp', split_axis=2, concat_axis=0, tiled=True)  260 us
    reduce_scatter x1, waiting for transfers between devices, attention_part(): return lax.psum_scatter(full_sum, 'dp', scatter_dimension=0, tiled=True)  128 us
    all_gather x1, waiting for transfers between devices, shards(): gathered = lax.all_gather(grad_out, 'tensor', axis=0, tiled=True)  125 us
    unnamed x1, other arithmetic  70.4 us
    unnamed x13, local copies, waits for them, and re-layouts  61 us
    broadcast_in_dim x1, local copies, waits for them, and re-layouts, module_part(): product[None]  27.6 us
    dot_general x3, matrix products, contract_rows(): lax.dot_general(left, right, (((0,), (0,)), ((), ())), preferred_element_...  15.2 us
  transfers between devices with their start and end apart: 3, of which 3 were waited for; matrix products, arithmetic and copies ran while one was open for 8% of the time, Pallas kernels for 0%

commit v1 on v0

v1 whole, which is shorter than its diff:
```python
import functools

import jax
import jax.numpy as jnp
from jax import lax
from jax.experimental import pallas as pl
from jax.experimental.pallas import tpu as pltpu
from jax.sharding import PartitionSpec as P

LANGS = 4
NX = 4
NC = 2
NH = 2
SUB = 4
BF = jnp.bfloat16
F32 = jnp.float32


def body(nz, ny, lang, hid, ctx, grad, out_m, out_a,
         stage, hext, hraw, hm, gbuf, relay, part, rbuf, obuf,
         ft, ftx, at, atx,
         a_s, a_r, h_s, h_r, hf_s, hf_r, hc_s, hc_r,
         e_s, e_r, ef_s, ef_r, y_s, y_r, g_s, g_r, z_s, z_r, o_s, o_r):
    ff, tok = hid.shape
    nctx = ctx.shape[1]
    fh, ch = ff // 2, nctx // 2
    hr = fh + ch
    rows = LANGS * fh + ch
    tt = grad.shape[0]
    pairs = nz // 2
    sub = rows // SUB
    split = (hr // 32) * 16

    dp = lax.axis_index("dp")
    ten = lax.axis_index("tensor")
    z = dp // (NX * NC)
    x = (dp // NC) % NX
    c = dp % NC
    h = ten // ny
    y = ten % ny
    zp = h * nz + z

    def dev(z_, x_, c_, h_, y_):
        return ((z_ * NX + x_) * NC + c_, h_ * ny + y_)

    def ring(place):
        place = lax.rem(place + 2 * NH * nz, NH * nz)
        return lax.rem(place, nz), place // nz

    def send(src, dst, ssem, rsem, where):
        return pltpu.make_async_remote_copy(
            src_ref=src, dst_ref=dst, send_sem=ssem, recv_sem=rsem,
            device_id=where, device_id_type=pl.DeviceIdType.MESH)

    xr, xl = lax.rem(x + 1, NX), lax.rem(x + NX - 1, NX)
    x2 = lax.rem(x + 2, NX)
    oc = 1 - c
    zu, hu = ring(zp + nz // 2)
    zd, hd = ring(zp - nz // 2)
    zn, zb = lax.rem(z + 1, nz), lax.rem(z + nz - 1, nz)

    barrier = pltpu.get_barrier_semaphore()
    friends = [dev(z, xr, 0, h, y), dev(z, xr, 1, h, y),
               dev(z, xl, 0, h, y), dev(z, xl, 1, h, y),
               dev(z, x2, c, h, y), dev(z, x, oc, h, y),
               dev(zu, x, c, hu, y), dev(zd, x, c, hd, y),
               dev(zn, x, c, h, y), dev(zb, x, c, h, y)]
    for d in range(1, ny):
        friends.append(dev(z, x, c, h, lax.rem(y + d, ny)))
    for f in friends:
        pl.semaphore_signal(barrier, inc=1, device_id=f,
                            device_id_type=pl.DeviceIdType.MESH)

    for k in range(NX):
        for p in range(pairs):
            for i, o in enumerate((nz - 1 - p, p)):
                lo = (o * NX + k) * 128
                stage[k, p, :, i * 128:(i + 1) * 128] = grad[:, lo:lo + 128]
    ctx_t = ctx[...].T
    for k in range(NC):
        hext[k, :fh, :] = hid[k * fh:(k + 1) * fh, :]
        hext[k, fh:, :] = ctx_t[k * ch:(k + 1) * ch, :]
    pl.semaphore_wait(barrier, len(friends))

    a = []
    for d in range(1, NX):
        k = lax.rem(x + d, NX)
        a.append(send(stage.at[k], gbuf.at[:, x, c, ten],
                      a_s.at[d - 1], a_r.at[d - 1], dev(z, k, c, h, y)))
        a[-1].start()
    h1 = []
    for i, k in enumerate((xr, xl)):
        for cc in range(NC):
            h1.append(send(hext.at[cc], hraw.at[x, c],
                           h_s.at[i, cc], h_r.at[i, c], dev(z, k, cc, h, y)))
            h1[-1].start()
    hc = send(hext.at[oc], hraw.at[x, c], hc_s.at[0], hc_r.at[0],
              dev(z, x, oc, h, y))
    hc.start()
    gbuf[:, x, c, ten] = stage[x]
    hraw[x, c] = hext[c]
    for cp in a:
        cp.wait_recv()

    e1, yo, yb = [], [], []
    for p in range(pairs):
        for i, (zz, hh) in enumerate(((zu, hu), (zd, hd))):
            e1.append(send(gbuf.at[p, pl.ds(2 * i, 2), c, ten], relay.at[p, i],
                           e_s.at[p, i], e_r.at[p, i], dev(zz, x, c, hh, y)))
            e1[-1].start()
        for d in range(1, ny):
            blk = gbuf.at[p, :, c, ten]
            yo.append(send(blk, blk, y_s.at[p, 0, d - 1], y_r.at[p, 0, d - 1],
                           dev(z, x, c, h, lax.rem(y + d, ny))))
            yo[-1].start()
    e2 = []
    for p in range(pairs):
        for i, (zz, hh, h0) in enumerate(((zu, hu, hd), (zd, hd, hu))):
            e1[p * 2 + i].wait_recv()
            e2.append(send(relay.at[p, i],
                           gbuf.at[p, pl.ds(2 * i, 2), c, h0 * ny + y],
                           ef_s.at[p, i], ef_r.at[p, i], dev(zz, x, c, hh, y)))
            e2[-1].start()
    h2 = []
    for i, (k, src) in enumerate(((xr, xl), (xl, xr))):
        for cc in range(NC):
            pltpu.make_async_remote_copy(
                src_ref=hext.at[cc], dst_ref=hraw.at[src, cc],
                send_sem=h_s.at[i, cc], recv_sem=h_r.at[i, cc],
                device_id=dev(z, src, cc, h, y),
                device_id_type=pl.DeviceIdType.MESH).wait_recv()
            r0, rn = (0, split) if i == 0 else (split, hr - split)
            blk = hraw.at[src, cc, pl.ds(r0, rn)]
            h2.append(send(blk, blk, hf_s.at[i, cc], hf_r.at[i, cc],
                           dev(z, k, c, h, y)))
            h2[-1].start()
    toth = (1 - h) * ny + y
    for p in range(pairs):
        e2[2 * p].wait_recv()
        e2[2 * p + 1].wait_recv()
        for d in range(1, ny):
            blk = gbuf.at[p, :, c, toth]
            yb.append(send(blk, blk, y_s.at[p, 1, d - 1], y_r.at[p, 1, d - 1],
                           dev(z, x, c, h, lax.rem(y + d, ny))))
            yb[-1].start()

    hc.wait_recv()
    for cp in h2:
        cp.wait_recv()

    def mask_rep(r, carry):
        xs, cs = r // NC, r % NC
        who = lang[z * (NX * NC) + r]
        at_col = pl.ds(pl.multiple_of(r * tok, tok), tok)
        val = hraw[xs, cs, :fh, :]
        for l in range(LANGS):
            keep = jnp.where(who == l, 1.0, 0.0).astype(F32)
            hm[l * fh:(l + 1) * fh, at_col] = (val * keep.astype(BF)).astype(BF)
        hm[LANGS * fh:, at_col] = hraw[xs, cs, fh:, :]
        return carry

    lax.fori_loop(0, NX * NC, mask_rep, 0)

    gc = []
    for p in range(pairs):
        for d in range(ny - 1):
            yo[p * (ny - 1) + d].wait_recv()
            yb[p * (ny - 1) + d].wait_recv()
        blk = gbuf.at[p, :, c]
        gc.append(send(blk, blk, g_s.at[p], g_r.at[p], dev(z, x, oc, h, y)))
        gc[-1].start()

    tile = rows // 3

    def pair(p):
        right = gbuf[p].reshape(NX * NC * tok, 256)

        def some_rows(i, carry):
            r = pl.ds(pl.multiple_of(i * tile, 16), tile)
            res = jnp.dot(hm[r, :], right, preferred_element_type=F32)
            part[nz - 1 - p, r, :] = res[:, :128]
            part[p, r, :] = res[:, 128:]
            return carry

        lax.fori_loop(0, rows // tile, some_rows, 0)

    def hop(way, o, q):
        r = pl.ds(q * sub, sub)
        zz = zn if way == 0 else zb
        return send(obuf.at[o, r], rbuf.at[way, o, r],
                    z_s.at[o, q], z_r.at[way, o, q], dev(zz, x, c, h, y))

    def chain(way, o):
        first = (z == 0) if way == 0 else (z == nz - 1)
        for q in range(SUB):
            r = pl.ds(q * sub, sub)
            cp = hop(way, o, q)

            @pl.when(jnp.logical_not(first))
            def _():
                cp.wait_recv()
                obuf[o, r, :] = (part[o, r, :] + rbuf[way, o, r, :].astype(F32)).astype(BF)

            @pl.when(first)
            def _():
                obuf[o, r, :] = part[o, r, :].astype(BF)

            cp.start()

    def slot(s, last):
        @pl.when(s >= z)
        def _():
            chain(0, nz - 1 + z - s)

        @pl.when(s >= nz - 1 - z)
        def _():
            chain(1, s - (nz - 1) + z)

    for s in range(nz - 1):
        if s < pairs:
            gc[s].wait_recv()
            pair(s)
        slot(s, False)

    for q in range(SUB):
        r = pl.ds(q * sub, sub)

        @pl.when(z > 0)
        def _():
            hop(0, z, q).wait_recv()
            part[z, r, :] = part[z, r, :] + rbuf[0, z, r, :].astype(F32)

        @pl.when(z < nz - 1)
        def _():
            hop(1, z, q).wait_recv()
            part[z, r, :] = part[z, r, :] + rbuf[1, z, r, :].astype(F32)

    for l in range(LANGS):
        ft[l] = part[z, l * fh:(l + 1) * fh, :].T.astype(BF)
    at[...] = part[z, LANGS * fh:, :].T
    mine = pl.ds(pl.multiple_of(c * 64, 64), 64)
    other = pl.ds(pl.multiple_of(oc * 64, 64), 64)
    s1 = send(ft.at[:, other], ftx, o_s.at[0], o_r.at[0], dev(z, x, oc, h, y))
    s2 = send(at.at[other], atx, o_s.at[1], o_r.at[1], dev(z, x, oc, h, y))
    s1.start()
    s2.start()

    for cp in a + h1 + [hc] + e1 + yo + e2 + h2 + yb + gc:
        cp.wait_send()

    def drain(o, carry):
        @pl.when(o != z)
        def _():
            for q in range(SUB):
                hop(0, o, q).wait_send()
        return carry

    lax.fori_loop(0, nz, drain, 0)
    s1.wait()
    s2.wait()
    low = c == 0
    for l in range(LANGS):
        me, it = ft[l, mine, :], ftx[l]
        out_m[l, :, :fh] = jnp.where(low, me, it)
        out_m[l, :, fh:] = jnp.where(low, it, me)
    me, it = at[mine, :], atx[...]
    out_a[:, :ch] = jnp.where(low, me, it)
    out_a[:, ch:] = jnp.where(low, it, me)


def shards(nz, ny, language, hidden, context, grad_out):
    tok, ff = hidden.shape
    nctx = context.shape[1]
    tt = grad_out.shape[0]
    fh, ch = ff // 2, nctx // 2
    hr, rows = fh + ch, LANGS * fh + ch
    pairs = nz // 2
    dma = pltpu.SemaphoreType.DMA
    vm = pl.BlockSpec(memory_space=pltpu.VMEM)
    y1 = max(ny - 1, 1)
    out_m, out_a = pl.pallas_call(
        functools.partial(body, nz, ny),
        out_shape=(jax.ShapeDtypeStruct((LANGS, 64, ff), BF),
                   jax.ShapeDtypeStruct((64, nctx), F32)),
        in_specs=[pl.BlockSpec(memory_space=pltpu.SMEM), vm, vm, vm],
        out_specs=(vm, vm),
        scratch_shapes=[
            pltpu.VMEM((NX, pairs, tt, 256), BF),
            pltpu.VMEM((NC, hr, tok), BF),
            pltpu.VMEM((NX, NC, hr, tok), BF),
            pltpu.VMEM((rows, NX * NC * tok), BF),
            pltpu.VMEM((pairs, NX, NC, NH * ny, tt, 256), BF),
            pltpu.VMEM((pairs, 2, 2, tt, 256), BF),
            pltpu.VMEM((nz, rows, 128), F32),
            pltpu.VMEM((2, nz, rows, 128), BF),
            pltpu.VMEM((nz, rows, 128), BF),
            pltpu.VMEM((LANGS, 128, fh), BF),
            pltpu.VMEM((LANGS, 64, fh), BF),
            pltpu.VMEM((128, ch), F32),
            pltpu.VMEM((64, ch), F32),
            dma((NX - 1,)), dma((NX - 1,)),
            dma((2, NC)), dma((2, NC)), dma((2, NC)), dma((2, NC)),
            dma((1,)), dma((1,)),
            dma((pairs, 2)), dma((pairs, 2)), dma((pairs, 2)), dma((pairs, 2)),
            dma((pairs, 2, y1)), dma((pairs, 2, y1)),
            dma((pairs,)), dma((pairs,)),
            dma((nz, SUB)), dma((2, nz, SUB)),
            dma((2,)), dma((2,)),
        ],
        compiler_params=pltpu.CompilerParams(
            collective_id=0, has_side_effects=True,
            vmem_limit_bytes=48 * 1024 * 1024),
        cost_estimate=pl.CostEstimate(
            flops=2 * rows * NX * NC * tok * nz * 128,
            bytes_accessed=4 * 1024 * 1024, transcendentals=0),
    )(language, hidden.T, context, grad_out)
    return jnp.swapaxes(out_m, 1, 2), out_a


def solution(mesh):
    nz = mesh.shape["dp"] // (NX * NC)
    ny = mesh.shape["tensor"] // NH
    return jax.shard_map(
        functools.partial(shards, nz, ny),
        mesh=mesh,
        in_specs=(P(), P("dp", "tensor"), P("dp", "tensor"), P(("dp", "tensor"), None)),
        out_specs=(P(None, "tensor", "dp"), P("dp", "tensor")),
        check_vma=False,
    )
```

time: 726 us -> 127 us (0.17); the launches traced: 713 us -> 127 us
  waiting for transfers between devices: 515 us -> 0 us
  Pallas kernels: 0 us -> 121 us
  local copies, waits for them, and re-layouts: 88.7 us -> 4.86 us
  other arithmetic: 70.4 us -> 0 us
  matrix products: 15.2 us -> 0 us
  between operations: 14.1 us -> 0.65 us
  starting transfers between devices: 10 us -> 0 us
    all_to_all x1 -> x0, waiting for transfers between devices: 260 us -> none  [module_part(): lax.all_to_all(product[None], 'dp', split_axis=2, concat_axis=0, tiled=True)]
    reduce_scatter x1 -> x0, waiting for transfers between devices: 128 us -> none  [attention_part(): return lax.psum_scatter(full_sum, 'dp', scatter_dimension=0, tiled=True)]
    all_gather x1 -> x0, waiting for transfers between devices: 125 us -> none  [shards(): gathered = lax.all_gather(grad_out, 'tensor', axis=0, tiled=True)]
    pallas_call x0 -> x1, Pallas kernels: none -> 121 us  [shards(): pl.pallas_call(functools.partial(body, nz, ny), out_shape=(jax.ShapeDtype...]
    unnamed x1 -> x0, other arithmetic: 70.4 us -> none
    unnamed x13 -> x10, local copies, waits for them, and re-layouts: 61 us -> 4.86 us
    broadcast_in_dim x1 -> x0, local copies, waits for them, and re-layouts: 27.6 us -> none  [module_part(): product[None]]
    dot_general x3 -> x0, matrix products: 15.2 us -> none  [contract_rows(): lax.dot_general(left, right, (((0,), (0,)), ((), ())), preferred_element_...]
  transfers between devices with their start and end apart: 3 -> 0, of which waited for: 3 -> 0; matrix products, arithmetic and copies ran while one was open for 8% -> 0% of each run, Pallas kernels for 0% -> 0%
where the time goes in v1:
time: 127 us
  Pallas kernels  121 us (95%)
  local copies, waits for them, and re-layouts  4.86 us (4%)
    pallas_call x1, Pallas kernels, shards(): pl.pallas_call(functools.partial(body, nz, ny), out_shape=(jax.ShapeDtype...  121 us
    unnamed x10, local copies, waits for them, and re-layouts  4.86 us

profile of v1, /device:TPU:1, one launch (start us, length us, event | category | flops | bytes accessed | tf_op | source)
XLA Modules:
  0.0 126.7 jit_solution(17161769700938673877)
XLA Ops:
  0.6 0.0 copy-start.3
  0.6 0.6 copy-done.3
  1.3 0.0 copy-start
  1.3 1.0 copy-done
  2.3 0.0 copy-start.1
  2.3 0.9 copy-done.1
  3.2 0.0 copy-start.2
  3.2 0.9 copy-done.2
  4.1 121.2 %shard_map.59 = (bf16[4,64,704]{2,1,0:T(8,128)(2,1)S(1)}, f32[64,256]{1,0:T(8,128)S(1)}) custom-call(s32[64]{0:T(128)S(1)} %copy-done.3, bf16[704,256]{1,0:T(8,128)(2,1)S(1)} %bitcast.3, bf16[256,256]{1,0:T(8,128)(2,1)S(1)} %copy-done.2, bf16[32,4096]{1,0:T(8,128)(2,1)S(1)} %copy-done.1), custom_call_target="tpu_custom_call" | custom-call | flops 6442450944 | bytes 4194304 | tf_op jit(solution)/shard_map/pallas_call | solution.py:281
  125.4 0.7 copy.8
  126.1 0.6 copy.9
Async XLA Ops:
  0.6 0.7 copy-start.3
  1.3 1.0 copy-start
  2.3 0.9 copy-start.1
  3.2 0.9 copy-start.2

commit v2 on v0

v2 whole, which is shorter than its diff:
```python
import functools

import jax
import jax.numpy as jnp
from jax import lax
from jax.experimental import pallas as pl
from jax.experimental.pallas import tpu as pltpu
from jax.sharding import PartitionSpec as P

LANGS = 4
NX = 4
NC = 2
NH = 2
BF = jnp.bfloat16
F32 = jnp.float32

ORDERS = {
    4: ("E0 E1 X C0", "E2 C1 M P0", "S0 E3 C2 P1", "S1 C3 P2 S2", "P3 W S3"),
    2: ("E0 X C0 E1", "M P0 S0 C1", "P1 W S1"),
    1: ("E0 X C0 M", "P0 W S0"),
}


def body(nz, ny, lang, hid, ctx, grad, out_m, out_a,
         graw, craw, own, hext, hraw, hm, gbuf, part, rbuf, obuf, fin, sx, acc, om, oa,
         l_s, a_s, a_r, e_s, e_r, h_s, h_r, hf_s, hf_r, hc_s, hc_r,
         y_s, y_r, g_s, g_r, z_s, z_r, f_s, f_r, o_s, o_r, w_s):
    ff, tok = hid.shape
    nctx = ctx.shape[1]
    fh, ch = ff // 2, nctx // 2
    hr = fh + ch
    np_, lp = part.shape[1], part.shape[3]
    pairs = nz // 2
    split = (hr // 32) * 16

    dp = lax.axis_index("dp")
    ten = lax.axis_index("tensor")
    z = dp // (NX * NC)
    x = (dp // NC) % NX
    c = dp % NC
    h = ten // ny
    y = ten % ny
    oc, oh = 1 - c, 1 - h
    toth = oh * ny + y

    def dev(z_, x_, c_, h_, y_):
        return ((z_ * NX + x_) * NC + c_, h_ * ny + y_)

    def send(src, dst, ssem, rsem, where):
        return pltpu.make_async_remote_copy(
            src_ref=src, dst_ref=dst, send_sem=ssem, recv_sem=rsem,
            device_id=where, device_id_type=pl.DeviceIdType.MESH)

    xs_at = [lax.rem(x + d, NX) for d in range(NX)]
    ys_at = [lax.rem(y + d, ny) for d in range(ny)]
    xr, xl = xs_at[1], xs_at[NX - 1]
    zn, zb = lax.rem(z + 1, nz), lax.rem(z + nz - 1, nz)

    barrier = pltpu.get_barrier_semaphore()
    friends = [dev(z, k, c, h, y) for k in xs_at[1:]]
    friends += [dev(z, k, oc, h, y) for k in (x, xr, xl)]
    friends += [dev(z, k, c, oh, y) for k in xs_at]
    friends += [dev(z, x, c, h, k) for k in ys_at[1:]]
    friends += [dev(k, x, cc, h, y) for k in (zn, zb) for cc in range(NC)]
    for f in friends:
        pl.semaphore_signal(barrier, inc=1, device_id=f,
                            device_id_type=pl.DeviceIdType.MESH)

    loads = [pltpu.make_async_copy(grad, graw, l_s.at[0]),
             pltpu.make_async_copy(ctx, craw, l_s.at[1])]
    for k in range(NC):
        loads.append(pltpu.make_async_copy(
            hid.at[pl.ds(k * fh, fh)], hext.at[k, pl.ds(0, fh)], l_s.at[2 + k]))
    for cp in loads:
        cp.start()

    loads[0].wait()
    for p in range(pairs):
        for k in range(NX):
            for i, o in enumerate((nz - 1 - p, p)):
                lo = (o * NX + k) * 128
                own[p, k, :, i * 128:(i + 1) * 128] = graw[:, lo:lo + 128]
    loads[1].wait()
    ctx_t = craw[...].T
    for k in range(NC):
        hext[k, fh:, :] = ctx_t[k * ch:(k + 1) * ch, :]
    loads[2].wait()
    loads[3].wait()
    pl.semaphore_wait(barrier, len(friends))

    e, a, yy = [], [], []

    def start_e(p):
        for d in range(NX):
            e.append((p, send(own.at[p, xs_at[d]], gbuf.at[p, x, c, ten],
                              e_s.at[p, d], e_r.at[p, d], dev(z, xs_at[d], c, oh, y))))
            e[-1][1].start()

    start_e(0)
    for d in range(1, NX):
        a.append(send(own.at[:, xs_at[d]], gbuf.at[:, x, c, ten],
                      a_s.at[d - 1], a_r.at[d - 1], dev(z, xs_at[d], c, h, y)))
        a[-1].start()
    h1 = []
    for i, k in enumerate((xr, xl)):
        for cc in range(NC):
            h1.append(send(hext.at[cc], hraw.at[x, c],
                           h_s.at[i, cc], h_r.at[i, c], dev(z, k, cc, h, y)))
            h1[-1].start()
    hc = send(hext.at[oc], hraw.at[x, c], hc_s.at[0], hc_r.at[0],
              dev(z, x, oc, h, y))
    hc.start()
    for p in range(1, pairs):
        start_e(p)
    gbuf[:, x, c, ten] = own[:, x]
    hraw[x, c] = hext[c]

    def start_y(p, w, t):
        blk = gbuf.at[p, :, c, t]
        for d in range(1, ny):
            yy.append((p, send(blk, blk, y_s.at[p, w, d - 1], y_r.at[p, w, d - 1],
                               dev(z, x, c, h, ys_at[d]))))
            yy[-1][1].start()

    for cp in a:
        cp.wait_recv()
    for p in range(pairs):
        start_y(p, 0, ten)

    def spread_y(p):
        for n, cp in e:
            if n == p:
                cp.wait_recv()
        start_y(p, 1, toth)

    gc = [None] * pairs

    def to_core(p):
        for n, cp in yy:
            if n == p:
                cp.wait_recv()
        blk = gbuf.at[p, :, c]
        gc[p] = send(blk, blk, g_s.at[p], g_r.at[p], dev(z, x, oc, h, y))
        gc[p].start()

    h2 = []

    def on_x():
        for i, (k, src) in enumerate(((xr, xl), (xl, xr))):
            for cc in range(NC):
                send(hext.at[cc], hraw.at[src, cc], h_s.at[i, cc], h_r.at[i, cc],
                     dev(z, src, cc, h, y)).wait_recv()
                r0, rn = (0, split) if i == 0 else (split, hr - split)
                blk = hraw.at[src, cc, pl.ds(r0, rn)]
                h2.append(send(blk, blk, hf_s.at[i, cc], hf_r.at[i, cc],
                               dev(z, k, c, h, y)))
                h2[-1].start()

    def mask_rep(r, carry):
        xs, cs = r // NC, r % NC
        who = lang[z * (NX * NC) + r]
        at_col = pl.ds(pl.multiple_of(r * tok, tok), tok)
        val = hraw[xs, cs, :fh, :]
        for l in range(LANGS):
            keep = jnp.where(who == l, 1.0, 0.0).astype(F32)
            hm[l * fh:(l + 1) * fh, at_col] = (val * keep.astype(BF)).astype(BF)
        hm[LANGS * fh:, at_col] = hraw[xs, cs, fh:, :]
        return carry

    def masked():
        hc.wait_recv()
        for cp in h2:
            cp.wait_recv()
        lax.fori_loop(0, NX * NC, mask_rep, 0)

    def pair(p):
        gc[p].wait_recv()
        right = gbuf[p].reshape(NX * NC * tok, 256)

        def some_rows(i, carry):
            r = pl.ds(pl.multiple_of(i * lp, lp), lp)
            res = jnp.dot(hm[r, :], right, preferred_element_type=F32).T
            part[nz - 1 - p, i] = res[:128]
            part[p, i] = res[128:]
            return carry

        lax.fori_loop(0, np_, some_rows, 0)

    def hop(way, o, q):
        return send(obuf.at[o, q], rbuf.at[way, o, q],
                    z_s.at[o, q], z_r.at[way, o, q],
                    dev(zn if way == 0 else zb, x, c, h, y))

    def last_hop(way, q, cc, o, cs):
        return send(obuf.at[o, q, pl.ds(64 * cc, 64)], fin.at[way, cs, q],
                    f_s.at[way, q, cc], f_r.at[way, q, cs],
                    dev(zn if way == 0 else zb, x, cc, h, y))

    def chain(way, o):
        first = (z == 0) if way == 0 else (z == nz - 1)
        last = (o == z + 1) if way == 0 else (o == z - 1)
        for q in range(np_):
            @pl.when(jnp.logical_not(first))
            def _():
                hop(way, o, q).wait_recv()
                obuf[o, q] = (part[o, q] + rbuf[way, o, q].astype(F32)).astype(BF)

            @pl.when(first)
            def _():
                obuf[o, q] = part[o, q].astype(BF)

            @pl.when(last)
            def _():
                for cc in range(NC):
                    last_hop(way, q, cc, o, c).start()

            @pl.when(jnp.logical_not(last))
            def _():
                hop(way, o, q).start()

    def slot(s):
        @pl.when(s >= z)
        def _():
            chain(0, nz - 1 + z - s)

        @pl.when(s >= nz - 1 - z)
        def _():
            chain(1, s - (nz - 1) + z)

    mine = pl.ds(pl.multiple_of(c * 64, 64), 64)
    other = pl.ds(pl.multiple_of(oc * 64, 64), 64)
    swap = send(part.at[z, :, other], sx, o_s.at[0], o_r.at[0], dev(z, x, oc, h, y))

    do = {"E": spread_y, "C": to_core, "X": on_x, "M": masked,
          "P": pair, "S": slot, "W": swap.start}
    for step in [w for group in ORDERS[pairs] for w in group.split()]:
        do[step[0]](*(int(v) for v in step[1:]))
    for s in range(pairs, nz - 1):
        slot(s)

    for cp in a + h1 + [hc] + h2 + gc:
        cp.wait_send()
    for n, cp in e + yy:
        cp.wait_send()

    swap.wait()
    low = c == 0
    writes = []
    for q in range(np_):
        one, two = part[z, q, mine, :], sx[q]
        acc[0, :, q * lp:(q + 1) * lp] = jnp.where(low, one, two)
        acc[1, :, q * lp:(q + 1) * lp] = jnp.where(low, two, one)
        for way, there in ((0, z > 0), (1, z < nz - 1)):
            @pl.when(there)
            def _():
                for cs in range(NC):
                    last_hop(way, q, cs, z, cs).wait_recv()
                    at_l = slice(q * lp, (q + 1) * lp)
                    acc[cs, :, at_l] = acc[cs, :, at_l] + fin[way, cs, q].astype(F32)

        for l in range(LANGS):
            if q * lp < (l + 1) * fh <= (q + 1) * lp:
                for cs in range(NC):
                    om[l, :, cs * fh:(cs + 1) * fh] = acc[cs, :, l * fh:(l + 1) * fh].astype(BF)
                writes.append(pltpu.make_async_copy(om.at[l], out_m.at[l], w_s.at[l]))
                writes[-1].start()
    for cs in range(NC):
        oa[:, cs * ch:(cs + 1) * ch] = acc[cs, :, LANGS * fh:]
    writes.append(pltpu.make_async_copy(oa, out_a, w_s.at[LANGS]))
    writes[-1].start()

    def drain(o, carry):
        @pl.when(jnp.logical_or(o > z + 1, o < z - 1))
        def _():
            for q in range(np_):
                hop(0, o, q).wait_send()
        return carry

    lax.fori_loop(0, nz, drain, 0)
    for q in range(np_):
        for way, there in ((0, z < nz - 1), (1, z > 0)):
            @pl.when(there)
            def _():
                for cc in range(NC):
                    last_hop(way, q, cc, z, c).wait_send()
    for cp in writes:
        cp.wait()


def shards(nz, ny, language, hidden, context, grad_out):
    tok, ff = hidden.shape
    nctx = context.shape[1]
    tt = grad_out.shape[0]
    fh, ch = ff // 2, nctx // 2
    hr, rows = fh + ch, LANGS * fh + ch
    np_ = 4 if rows % 512 == 0 else 3
    lp = rows // np_
    pairs = nz // 2
    dma = pltpu.SemaphoreType.DMA
    hbm = pl.BlockSpec(memory_space=pltpu.HBM)
    y1 = max(ny - 1, 1)
    out_m, out_a = pl.pallas_call(
        functools.partial(body, nz, ny),
        out_shape=(jax.ShapeDtypeStruct((LANGS, 64, ff), BF),
                   jax.ShapeDtypeStruct((64, nctx), F32)),
        in_specs=[pl.BlockSpec(memory_space=pltpu.SMEM), hbm, hbm, hbm],
        out_specs=(hbm, hbm),
        scratch_shapes=[
            pltpu.VMEM((tt, nz * NX * 128), BF),
            pltpu.VMEM((tok, nctx), BF),
            pltpu.VMEM((pairs, NX, tt, 256), BF),
            pltpu.VMEM((NC, hr, tok), BF),
            pltpu.VMEM((NX, NC, hr, tok), BF),
            pltpu.VMEM((rows, NX * NC * tok), BF),
            pltpu.VMEM((pairs, NX, NC, NH * ny, tt, 256), BF),
            pltpu.VMEM((nz, np_, 128, lp), F32),
            pltpu.VMEM((2, nz, np_, 128, lp), BF),
            pltpu.VMEM((nz, np_, 128, lp), BF),
            pltpu.VMEM((2, NC, np_, 64, lp), BF),
            pltpu.VMEM((np_, 64, lp), F32),
            pltpu.VMEM((NC, 64, rows), F32),
            pltpu.VMEM((LANGS, 64, ff), BF),
            pltpu.VMEM((64, nctx), F32),
            dma((2 + NC,)),
            dma((NX - 1,)), dma((NX - 1,)),
            dma((pairs, NX)), dma((pairs, NX)),
            dma((2, NC)), dma((2, NC)), dma((2, NC)), dma((2, NC)),
            dma((1,)), dma((1,)),
            dma((pairs, 2, y1)), dma((pairs, 2, y1)),
            dma((pairs,)), dma((pairs,)),
            dma((nz, np_)), dma((2, nz, np_)),
            dma((2, np_, NC)), dma((2, np_, NC)),
            dma((1,)), dma((1,)),
            dma((1 + LANGS,)),
        ],
        compiler_params=pltpu.CompilerParams(
            collective_id=0, has_side_effects=True,
            vmem_limit_bytes=60 * 1024 * 1024),
        cost_estimate=pl.CostEstimate(
            flops=2 * rows * NX * NC * tok * nz * 128,
            bytes_accessed=4 * 1024 * 1024, transcendentals=0),
    )(language, hidden.T, context, grad_out)
    return jnp.swapaxes(out_m, 1, 2), out_a


def solution(mesh):
    nz = mesh.shape["dp"] // (NX * NC)
    ny = mesh.shape["tensor"] // NH
    return jax.shard_map(
        functools.partial(shards, nz, ny),
        mesh=mesh,
        in_specs=(P(), P("dp", "tensor"), P("dp", "tensor"), P(("dp", "tensor"), None)),
        out_specs=(P(None, "tensor", "dp"), P("dp", "tensor")),
        check_vma=False,
    )
```

time: 726 us -> 116 us (0.16); the launches traced: 713 us -> 115 us
  waiting for transfers between devices: 515 us -> 0 us
  Pallas kernels: 0 us -> 112 us
  local copies, waits for them, and re-layouts: 88.7 us -> 2.43 us
  other arithmetic: 70.4 us -> 0 us
  matrix products: 15.2 us -> 0 us
  between operations: 14.1 us -> 0.65 us
  starting transfers between devices: 10 us -> 0 us
    all_to_all x1 -> x0, waiting for transfers between devices: 260 us -> none  [module_part(): lax.all_to_all(product[None], 'dp', split_axis=2, concat_axis=0, tiled=True)]
    reduce_scatter x1 -> x0, waiting for transfers between devices: 128 us -> none  [attention_part(): return lax.psum_scatter(full_sum, 'dp', scatter_dimension=0, tiled=True)]
    all_gather x1 -> x0, waiting for transfers between devices: 125 us -> none  [shards(): gathered = lax.all_gather(grad_out, 'tensor', axis=0, tiled=True)]
    pallas_call x0 -> x1, Pallas kernels: none -> 112 us  [shards(): pl.pallas_call(functools.partial(body, nz, ny), out_shape=(jax.ShapeDtype...]
    unnamed x1 -> x0, other arithmetic: 70.4 us -> none
    unnamed x13 -> x4, local copies, waits for them, and re-layouts: 61 us -> 2.43 us
    broadcast_in_dim x1 -> x0, local copies, waits for them, and re-layouts: 27.6 us -> none  [module_part(): product[None]]
    dot_general x3 -> x0, matrix products: 15.2 us -> none  [contract_rows(): lax.dot_general(left, right, (((0,), (0,)), ((), ())), preferred_element_...]
  transfers between devices with their start and end apart: 3 -> 0, of which waited for: 3 -> 0; matrix products, arithmetic and copies ran while one was open for 8% -> 0% of each run, Pallas kernels for 0% -> 0%
where the time goes in v2:
time: 116 us; the launch traced here: 115 us
  Pallas kernels  112 us (97%)
  local copies, waits for them, and re-layouts  2.43 us (2%)
    pallas_call x1, Pallas kernels, shards(): pl.pallas_call(functools.partial(body, nz, ny), out_shape=(jax.ShapeDtype...  112 us
    unnamed x4, local copies, waits for them, and re-layouts  2.43 us

profile of v2, /device:TPU:1, one launch (start us, length us, event | category | flops | bytes accessed | tf_op | source)
XLA Modules:
  0.0 115.5 jit_solution(16101200565085714759)
XLA Ops:
  0.6 112.4 %shard_map.59 = (bf16[4,64,704]{2,1,0:T(8,128)(2,1)}, f32[64,256]{1,0:T(8,128)}) custom-call(s32[64]{0:T(128)} %lang.1, bf16[704,256]{1,0:T(8,128)(2,1)} %bitcast.3, bf16[256,256]{1,0:T(8,128)(2,1)} %ctx.1, bf16[32,4096]{1,0:T(8,128)(2,1)} %grad.1), custom_call_target="tpu_custom_call" | custom-call | flops 6442450944 | bytes 4194304 | tf_op jit(solution)/shard_map/pallas_call | solution.py:302
  113.0 0.0 copy-start
  113.0 1.8 %copy.8 = bf16[4,704,64]{1,2,0:T(8,128)(2,1)} copy(bf16[4,704,64]{1,2,0:T(8,128)(2,1)} %bitcast.2) | data formatting | bytes 720896
  114.8 0.0 copy-done
  114.8 0.6 copy.9
Async XLA Ops:
  113.0 1.8 %copy-start = (f32[64,256]{1,0:T(8,128)S(1)}, f32[64,256]{1,0:T(8,128)}, u32[]{:S(2)}) copy-start(f32[64,256]{1,0:T(8,128)} %get-tuple-element.9) | copy-start | bytes 196612

commit v3 on v2

--- a/solution.py
+++ b/solution.py
@@ -15,9 +15,9 @@
 F32 = jnp.float32
 
 ORDERS = {
-    4: ("E0 E1 X C0", "E2 C1 M P0", "S0 E3 C2 P1", "S1 C3 P2 S2", "P3 W S3"),
-    2: ("E0 X C0 E1", "M P0 S0 C1", "P1 W S1"),
-    1: ("E0 X C0 M", "P0 W S0"),
+    4: (4, 4, "X M E0 E1", "C0 N E2 C1", "P0 E3 C2 P1", "S1 C3 P2 S2", "P3 W S3"),
+    2: (1, 1, "E0 X K1 Y1", "C0 M N P0", "E1 C1 P1 W", "S1"),
+    1: (1, 1, "E0 X C0 M", "N P0 W"),
 }
 
 
@@ -56,6 +56,14 @@
     xr, xl = xs_at[1], xs_at[NX - 1]
     zn, zb = lax.rem(z + 1, nz), lax.rem(z + nz - 1, nz)
 
+    loads = [pltpu.make_async_copy(grad, graw, l_s.at[0]),
+             pltpu.make_async_copy(ctx, craw, l_s.at[1])]
+    for k in range(NC):
+        loads.append(pltpu.make_async_copy(
+            hid.at[pl.ds(k * fh, fh)], hext.at[k, pl.ds(0, fh)], l_s.at[2 + k]))
+    for cp in loads:
+        cp.start()
+
     barrier = pltpu.get_barrier_semaphore()
     friends = [dev(z, k, c, h, y) for k in xs_at[1:]]
     friends += [dev(z, k, oc, h, y) for k in (x, xr, xl)]
@@ -66,41 +74,35 @@
         pl.semaphore_signal(barrier, inc=1, device_id=f,
                             device_id_type=pl.DeviceIdType.MESH)
 
-    loads = [pltpu.make_async_copy(grad, graw, l_s.at[0]),
-             pltpu.make_async_copy(ctx, craw, l_s.at[1])]
-    for k in range(NC):
-        loads.append(pltpu.make_async_copy(
-            hid.at[pl.ds(k * fh, fh)], hext.at[k, pl.ds(0, fh)], l_s.at[2 + k]))
-    for cp in loads:
-        cp.start()
-
     loads[0].wait()
     for p in range(pairs):
         for k in range(NX):
             for i, o in enumerate((nz - 1 - p, p)):
                 lo = (o * NX + k) * 128
                 own[p, k, :, i * 128:(i + 1) * 128] = graw[:, lo:lo + 128]
+    pl.semaphore_wait(barrier, len(friends))
+
+    e, a, yy = [], [], []
+
+    def start_e(p):
+        for d in range(NX):
+            e.append((p, send(own.at[p, xs_at[d]], gbuf.at[p, x, c, ten],
+                              e_s.at[p, d], e_r.at[p, d], dev(z, xs_at[d], c, oh, y))))
+            e[-1][1].start()
+
+    order = ORDERS[pairs]
+    for p in range(order[0]):
+        start_e(p)
+    for d in range(1, NX):
+        a.append(send(own.at[:, xs_at[d]], gbuf.at[:, x, c, ten],
+                      a_s.at[d - 1], a_r.at[d - 1], dev(z, xs_at[d], c, h, y)))
+        a[-1].start()
     loads[1].wait()
     ctx_t = craw[...].T
     for k in range(NC):
         hext[k, fh:, :] = ctx_t[k * ch:(k + 1) * ch, :]
     loads[2].wait()
     loads[3].wait()
-    pl.semaphore_wait(barrier, len(friends))
-
-    e, a, yy = [], [], []
-
-    def start_e(p):
-        for d in range(NX):
-            e.append((p, send(own.at[p, xs_at[d]], gbuf.at[p, x, c, ten],
-                              e_s.at[p, d], e_r.at[p, d], dev(z, xs_at[d], c, oh, y))))
-            e[-1][1].start()
-
-    start_e(0)
-    for d in range(1, NX):
-        a.append(send(own.at[:, xs_at[d]], gbuf.at[:, x, c, ten],
-                      a_s.at[d - 1], a_r.at[d - 1], dev(z, xs_at[d], c, h, y)))
-        a[-1].start()
     h1 = []
     for i, k in enumerate((xr, xl)):
         for cc in range(NC):
@@ -110,8 +112,6 @@
     hc = send(hext.at[oc], hraw.at[x, c], hc_s.at[0], hc_r.at[0],
               dev(z, x, oc, h, y))
     hc.start()
-    for p in range(1, pairs):
-        start_e(p)
     gbuf[:, x, c, ten] = own[:, x]
     hraw[x, c] = hext[c]
 
@@ -124,7 +124,7 @@
 
     for cp in a:
         cp.wait_recv()
-    for p in range(pairs):
+    for p in range(order[1]):
         start_y(p, 0, ten)
 
     def spread_y(p):
@@ -156,8 +156,8 @@
                                dev(z, k, c, h, y)))
                 h2[-1].start()
 
-    def mask_rep(r, carry):
-        xs, cs = r // NC, r % NC
+    def mask_rep(xs, cs):
+        r = xs * NC + cs
         who = lang[z * (NX * NC) + r]
         at_col = pl.ds(pl.multiple_of(r * tok, tok), tok)
         val = hraw[xs, cs, :fh, :]
@@ -165,13 +165,21 @@
             keep = jnp.where(who == l, 1.0, 0.0).astype(F32)
             hm[l * fh:(l + 1) * fh, at_col] = (val * keep.astype(BF)).astype(BF)
         hm[LANGS * fh:, at_col] = hraw[xs, cs, fh:, :]
-        return carry
-
-    def masked():
+
+    def mask_near():
         hc.wait_recv()
+
+        def some(i, carry):
+            mask_rep(lax.rem(x + (NX - 1) + i // NC, NX), i % NC)
+            return carry
+
+        lax.fori_loop(0, (NX - 1) * NC, some, 0)
+
+    def mask_far():
         for cp in h2:
             cp.wait_recv()
-        lax.fori_loop(0, NX * NC, mask_rep, 0)
+        for cs in range(NC):
+            mask_rep(xs_at[2], cs)
 
     def pair(p):
         gc[p].wait_recv()
@@ -182,6 +190,14 @@
             res = jnp.dot(hm[r, :], right, preferred_element_type=F32).T
             part[nz - 1 - p, i] = res[:128]
             part[p, i] = res[128:]
+            if p == 0:
+                @pl.when(z == 0)
+                def _():
+                    chain_piece(0, nz - 1, i)
+
+                @pl.when(z == nz - 1)
+                def _():
+                    chain_piece(1, 0, i)
             return carry
 
         lax.fori_loop(0, np_, some_rows, 0)
@@ -196,46 +212,48 @@
                     f_s.at[way, q, cc], f_r.at[way, q, cs],
                     dev(zn if way == 0 else zb, x, cc, h, y))
 
-    def chain(way, o):
+    def chain_piece(way, o, q):
         first = (z == 0) if way == 0 else (z == nz - 1)
         last = (o == z + 1) if way == 0 else (o == z - 1)
-        for q in range(np_):
-            @pl.when(jnp.logical_not(first))
-            def _():
-                hop(way, o, q).wait_recv()
-                obuf[o, q] = (part[o, q] + rbuf[way, o, q].astype(F32)).astype(BF)
-
-            @pl.when(first)
-            def _():
-                obuf[o, q] = part[o, q].astype(BF)
-
-            @pl.when(last)
-            def _():
-                for cc in range(NC):
-                    last_hop(way, q, cc, o, c).start()
-
-            @pl.when(jnp.logical_not(last))
-            def _():
-                hop(way, o, q).start()
+
+        @pl.when(jnp.logical_not(first))
+        def _():
+            hop(way, o, q).wait_recv()
+            obuf[o, q] = (part[o, q] + rbuf[way, o, q].astype(F32)).astype(BF)
+
+        @pl.when(first)
+        def _():
+            obuf[o, q] = part[o, q].astype(BF)
+
+        @pl.when(last)
+        def _():
+            for cc in range(NC):
+                last_hop(way, q, cc, o, c).start()
+
+        @pl.when(jnp.logical_not(last))
+        def _():
+            hop(way, o, q).start()
 
     def slot(s):
         @pl.when(s >= z)
         def _():
-            chain(0, nz - 1 + z - s)
+            for q in range(np_):
+                chain_piece(0, nz - 1 + z - s, q)
 
         @pl.when(s >= nz - 1 - z)
         def _():
-            chain(1, s - (nz - 1) + z)
+            for q in range(np_):
+                chain_piece(1, s - (nz - 1) + z, q)
 
     mine = pl.ds(pl.multiple_of(c * 64, 64), 64)
     other = pl.ds(pl.multiple_of(oc * 64, 64), 64)
     swap = send(part.at[z, :, other], sx, o_s.at[0], o_r.at[0], dev(z, x, oc, h, y))
 
-    do = {"E": spread_y, "C": to_core, "X": on_x, "M": masked,
+    do = {"K": start_e, "Y": lambda p: start_y(p, 0, ten), "E": spread_y, "C": to_core, "X": on_x, "M": mask_near, "N": mask_far,
           "P": pair, "S": slot, "W": swap.start}
-    for step in [w for group in ORDERS[pairs] for w in group.split()]:
+    for step in [w for group in order[2:] for w in group.split()]:
         do[step[0]](*(int(v) for v in step[1:]))
-    for s in range(pairs, nz - 1):
+    for s in range(max(pairs, 1), nz - 1):
         slot(s)
 
     for cp in a + h1 + [hc] + h2 + gc:

time: 116 us -> 113 us (0.974)
  Pallas kernels: 112 us -> 110 us
    pallas_call x1, Pallas kernels: 112 us -> 110 us  [shards(): pl.pallas_call(functools.partial(body, nz, ny), out_shape=(jax.ShapeDtype...]
where the time goes in v3:
time: 113 us
  Pallas kernels  110 us (97%)
  local copies, waits for them, and re-layouts  2.43 us (2%)
    pallas_call x1, Pallas kernels, shards(): pl.pallas_call(functools.partial(body, nz, ny), out_shape=(jax.ShapeDtype...  110 us
    unnamed x4, local copies, waits for them, and re-layouts  2.43 us

profile of v3, /device:TPU:1, one launch (start us, length us, event | category | flops | bytes accessed | tf_op | source)
XLA Modules:
  0.0 112.7 jit_solution(7952660078416070879)
XLA Ops:
  0.6 109.7 %shard_map.59 = (bf16[4,64,704]{2,1,0:T(8,128)(2,1)}, f32[64,256]{1,0:T(8,128)}) custom-call(s32[64]{0:T(128)} %lang.1, bf16[704,256]{1,0:T(8,128)(2,1)} %bitcast.3, bf16[256,256]{1,0:T(8,128)(2,1)} %ctx.1, bf16[32,4096]{1,0:T(8,128)(2,1)} %grad.1), custom_call_target="tpu_custom_call" | custom-call | flops 6442450944 | bytes 4194304 | tf_op jit(solution)/shard_map/pallas_call | solution.py:320
  110.3 0.0 copy-start
  110.3 1.8 %copy.8 = bf16[4,704,64]{1,2,0:T(8,128)(2,1)} copy(bf16[4,704,64]{1,2,0:T(8,128)(2,1)} %bitcast.2) | data formatting | bytes 720896
  112.1 0.0 copy-done
  112.1 0.6 copy.9
Async XLA Ops:
  110.3 1.8 %copy-start = (f32[64,256]{1,0:T(8,128)S(1)}, f32[64,256]{1,0:T(8,128)}, u32[]{:S(2)}) copy-start(f32[64,256]{1,0:T(8,128)} %get-tuple-element.9) | copy-start | bytes 196612

commit v4 on v3

--- a/solution.py
+++ b/solution.py
@@ -15,7 +15,7 @@
 F32 = jnp.float32
 
 ORDERS = {
-    4: (4, 4, "X M E0 E1", "C0 N E2 C1", "P0 E3 C2 P1", "S1 C3 P2 S2", "P3 W S3"),
+    4: (4, 4, "F0 F1 F2 F3", "X M E0 E1", "C0 N E2 C1", "P0 E3 C2 P1", "S1 C3 P2 S2", "P3 W S3"),
     2: (1, 1, "E0 X K1 Y1", "C0 M N P0", "E1 C1 P1 W", "S1"),
     1: (1, 1, "E0 X C0 M", "N P0 W"),
 }
@@ -82,7 +82,7 @@
                 own[p, k, :, i * 128:(i + 1) * 128] = graw[:, lo:lo + 128]
     pl.semaphore_wait(barrier, len(friends))
 
-    e, a, yy = [], [], []
+    e, a, yy, yo = [], [], [], []
 
     def start_e(p):
         for d in range(NX):
@@ -118,8 +118,21 @@
     def start_y(p, w, t):
         blk = gbuf.at[p, :, c, t]
         for d in range(1, ny):
-            yy.append((p, send(blk, blk, y_s.at[p, w, d - 1], y_r.at[p, w, d - 1],
+            if w == 0 and ny == 4 and d == 2:
+                continue
+            (yo if w == 0 and ny == 4 else yy).append((p, send(blk, blk, y_s.at[p, w, d - 1], y_r.at[p, w, d - 1],
                                dev(z, x, c, h, ys_at[d]))))
+            (yo if w == 0 and ny == 4 else yy)[-1][1].start()
+
+    def on_y(p):
+        for n, cp in yo:
+            if n == p:
+                cp.wait_recv()
+        for i, (to, src) in enumerate(((1, 3), (3, 1))):
+            blk = gbuf.at[p, pl.ds(2 * i, 2), c, h * ny + ys_at[src]]
+            k = (1, 3)[i]
+            yy.append((p, send(blk, blk, y_s.at[p, 0, k], y_r.at[p, 0, k],
+                               dev(z, x, c, h, ys_at[to]))))
             yy[-1][1].start()
 
     for cp in a:
@@ -249,7 +262,7 @@
     other = pl.ds(pl.multiple_of(oc * 64, 64), 64)
     swap = send(part.at[z, :, other], sx, o_s.at[0], o_r.at[0], dev(z, x, oc, h, y))
 
-    do = {"K": start_e, "Y": lambda p: start_y(p, 0, ten), "E": spread_y, "C": to_core, "X": on_x, "M": mask_near, "N": mask_far,
+    do = {"K": start_e, "Y": lambda p: start_y(p, 0, ten), "E": spread_y, "C": to_core, "X": on_x, "F": on_y, "M": mask_near, "N": mask_far,
           "P": pair, "S": slot, "W": swap.start}
     for step in [w for group in order[2:] for w in group.split()]:
         do[step[0]](*(int(v) for v in step[1:]))
@@ -258,7 +271,7 @@
 
     for cp in a + h1 + [hc] + h2 + gc:
         cp.wait_send()
-    for n, cp in e + yy:
+    for n, cp in e + yy + yo:
         cp.wait_send()
 
     swap.wait()
@@ -316,7 +329,7 @@
     pairs = nz // 2
     dma = pltpu.SemaphoreType.DMA
     hbm = pl.BlockSpec(memory_space=pltpu.HBM)
-    y1 = max(ny - 1, 1)
+    y1 = max(ny, 1)
     out_m, out_a = pl.pallas_call(
         functools.partial(body, nz, ny),
         out_shape=(jax.ShapeDtypeStruct((LANGS, 64, ff), BF),

time: 113 us -> 113 us (level)
  no operation moved by 1% of the time
where the time goes in v4:
time: 113 us
  Pallas kernels  110 us (97%)
  local copies, waits for them, and re-layouts  2.43 us (2%)
    pallas_call x1, Pallas kernels, shards(): pl.pallas_call(functools.partial(body, nz, ny), out_shape=(jax.ShapeDtype...  110 us
    unnamed x4, local copies, waits for them, and re-layouts  2.43 us

profile of v4, /device:TPU:1, one launch (start us, length us, event | category | flops | bytes accessed | tf_op | source)
XLA Modules:
  0.0 112.9 jit_solution(9496382895848609295)
XLA Ops:
  0.6 109.8 %shard_map.59 = (bf16[4,64,704]{2,1,0:T(8,128)(2,1)}, f32[64,256]{1,0:T(8,128)}) custom-call(s32[64]{0:T(128)} %lang.1, bf16[704,256]{1,0:T(8,128)(2,1)} %bitcast.3, bf16[256,256]{1,0:T(8,128)(2,1)} %ctx.1, bf16[32,4096]{1,0:T(8,128)(2,1)} %grad.1), custom_call_target="tpu_custom_call" | custom-call | flops 6442450944 | bytes 4194304 | tf_op jit(solution)/shard_map/pallas_call | solution.py:333
  110.4 0.0 copy-start
  110.5 1.8 %copy.8 = bf16[4,704,64]{1,2,0:T(8,128)(2,1)} copy(bf16[4,704,64]{1,2,0:T(8,128)(2,1)} %bitcast.2) | data formatting | bytes 720896
  112.3 0.0 copy-done
  112.3 0.6 copy.9
Async XLA Ops:
  110.4 1.8 %copy-start = (f32[64,256]{1,0:T(8,128)S(1)}, f32[64,256]{1,0:T(8,128)}, u32[]{:S(2)}) copy-start(f32[64,256]{1,0:T(8,128)} %get-tuple-element.9) | copy-start | bytes 196612

commit v5 on v4

--- a/solution.py
+++ b/solution.py
@@ -203,14 +203,15 @@
             res = jnp.dot(hm[r, :], right, preferred_element_type=F32).T
             part[nz - 1 - p, i] = res[:128]
             part[p, i] = res[128:]
-            if p == 0:
-                @pl.when(z == 0)
-                def _():
-                    chain_piece(0, nz - 1, i)
-
-                @pl.when(z == nz - 1)
-                def _():
-                    chain_piece(1, 0, i)
+
+            @pl.when(z == 0)
+            def _():
+                chain_piece(0, nz - 1 - p, i)
+
+            @pl.when(z == nz - 1)
+            def _():
+                chain_piece(1, p, i)
+
             return carry
 
         lax.fori_loop(0, np_, some_rows, 0)
@@ -248,12 +249,14 @@
             hop(way, o, q).start()
 
     def slot(s):
-        @pl.when(s >= z)
+        inner = jnp.logical_or(s >= pairs, jnp.logical_and(z > 0, z < nz - 1))
+
+        @pl.when(jnp.logical_and(s >= z, inner))
         def _():
             for q in range(np_):
                 chain_piece(0, nz - 1 + z - s, q)
 
-        @pl.when(s >= nz - 1 - z)
+        @pl.when(jnp.logical_and(s >= nz - 1 - z, inner))
         def _():
             for q in range(np_):
                 chain_piece(1, s - (nz - 1) + z, q)

time: 113 us -> 113 us (level)
  no operation moved by 1% of the time
where the time goes in v5:
time: 113 us
  Pallas kernels  110 us (97%)
  local copies, waits for them, and re-layouts  2.43 us (2%)
    pallas_call x1, Pallas kernels, shards(): pl.pallas_call(functools.partial(body, nz, ny), out_shape=(jax.ShapeDtype...  110 us
    unnamed x4, local copies, waits for them, and re-layouts  2.43 us

profile of v5, /device:TPU:1, one launch (start us, length us, event | category | flops | bytes accessed | tf_op | source)
XLA Modules:
  0.0 112.9 jit_solution(1871717604003071193)
XLA Ops:
  0.6 109.8 %shard_map.59 = (bf16[4,64,704]{2,1,0:T(8,128)(2,1)}, f32[64,256]{1,0:T(8,128)}) custom-call(s32[64]{0:T(128)} %lang.1, bf16[704,256]{1,0:T(8,128)(2,1)} %bitcast.3, bf16[256,256]{1,0:T(8,128)(2,1)} %ctx.1, bf16[32,4096]{1,0:T(8,128)(2,1)} %grad.1), custom_call_target="tpu_custom_call" | custom-call | flops 6442450944 | bytes 4194304 | tf_op jit(solution)/shard_map/pallas_call | solution.py:336
  110.4 0.0 copy-start
  110.5 1.8 %copy.8 = bf16[4,704,64]{1,2,0:T(8,128)(2,1)} copy(bf16[4,704,64]{1,2,0:T(8,128)(2,1)} %bitcast.2) | data formatting | bytes 720896
  112.3 0.0 copy-done
  112.3 0.6 copy.9
Async XLA Ops:
  110.4 1.8 %copy-start = (f32[64,256]{1,0:T(8,128)S(1)}, f32[64,256]{1,0:T(8,128)}, u32[]{:S(2)}) copy-start(f32[64,256]{1,0:T(8,128)} %get-tuple-element.9) | copy-start | bytes 196612
